TPU v7x, 256 devices: a whole 4x4x8 slice. The times are simulated.
256 devices in a mesh: pair: 4 (over x), row: 64 (over z, y, core).
Axes of the slice: x: 4, y: 4, z: 8, core: 2. Of those that a mesh axis runs over, the one named last changes fastest.
Arguments:
- matrix: float32 [16384, 4096], P('row', 'pair'), may hold values from -18 to 18, as said below
- plan: int32 [2, 8], replicated, may hold values from 0 to 7, each once within a row
Outputs:
- rotated: float32 [16384, 4096], P('row', 'pair')
Inputs may be any that keep to these rules, and one draw needn't show every extreme that they name: `matrix`: an entry's magnitude is at most 18. `plan`: each row names every block number once.
All inputs are finite; a program needn't handle non-finite values.
Results may differ from a plain program's by a relative error of at most 0.0004.
Values sent between devices are 32-bit elements; how exact they have to be, the bound alone decides.
A program may use at most 128 MiB of HBM per device.

v0:
```python
import functools
import itertools

import jax
import jax.numpy as jnp
from jax import lax
from jax.experimental import pallas as pl
from jax.experimental.pallas import tpu as pltpu
from jax.sharding import PartitionSpec as P

F32 = jnp.float32
BF = jnp.bfloat16
MESH = pl.DeviceIdType.MESH
OFF = [(i, j) for i in range(8) for j in range(i + 1, 8)]
NZ, NY = 8, 4
HALF, PA, PB = 2048, 1536, 512
YA, ZA, ZB, YB = PA // NY, PA // NY // NZ, PB // NZ, PB // NZ // NY
ZORDER = (4, 3, 5, 2, 6, 1, 7)


def split(x):
    hi = x.astype(BF)
    return hi, (x - hi.astype(F32)).astype(BF)


def dot(a, b):
    return jnp.dot(a, b, preferred_element_type=F32)


def iotas(n, m):
    shape = (n, m)
    return lax.broadcasted_iota(jnp.int32, shape, 0), lax.broadcasted_iota(jnp.int32, shape, 1)


def vmem_call(kern, outs, n_smem, scratch, name, *args):
    vm = pl.BlockSpec(memory_space=pltpu.VMEM)
    sm = pl.BlockSpec(memory_space=pltpu.SMEM)
    return pl.pallas_call(
        kern,
        out_shape=outs,
        in_specs=[sm] * n_smem + [vm] * (len(args) - n_smem),
        out_specs=jax.tree.map(lambda _: vm, outs),
        scratch_shapes=scratch,
        compiler_params=pltpu.CompilerParams(vmem_limit_bytes=32 * 2**20),
        name=name,
    )(*args)


def load_pair(t_ref, parts, dst, row0):
    if len(parts) == 1:
        dst[row0:row0 + 256, :] = parts[0][...]
        return
    at = t_ref[4] * 512
    dst[row0:row0 + 256, pl.ds(pl.multiple_of(at, 512), 512)] = parts[0][...]
    dst[row0:row0 + 256, pl.ds(pl.multiple_of(512 - at, 512), 512)] = parts[1][...]


def gram_kern(n_parts, t_ref, *refs):
    parts = refs[:n_parts]
    g_ref, x_ref, ph, plo, th, tl = refs[n_parts:]
    load_pair(t_ref, parts, x_ref, 0)
    for c in range(0, 1024, 256):
        x = x_ref[:, c:c + 256]
        ph[:, c:c + 256], plo[:, c:c + 256] = split(x)
        th[c:c + 256, :], tl[c:c + 256, :] = split(x.T)
    bi, bj = iotas(128, 128)
    for i in range(4):
        r = slice(256 * i, 256 * i + 256)
        for j in range(i, 4):
            c = slice(256 * j, 256 * j + 256)
            g = dot(th[r, :], ph[:, c]) + (dot(th[r, :], plo[:, c]) + dot(tl[r, :], ph[:, c]))
            for u in range(2):
                for v in range(2):
                    if (2 * i + u, 2 * j + v) in OFF:
                        n = 128 * OFF.index((2 * i + u, 2 * j + v))
                        g_ref[n:n + 128, :] = g[128 * u:128 * u + 128, 128 * v:128 * v + 128]
            if i == j:
                n = 128 * (28 + i)
                g_ref[n:n + 128, :] = jnp.where(bj > bi, g[:128, :128], g[128:, 128:])


def gram(t, parts):
    return vmem_call(
        functools.partial(gram_kern, len(parts)),
        jax.ShapeDtypeStruct((4096, 128), F32),
        1,
        [pltpu.VMEM((256, 1024), F32)] + [pltpu.VMEM((256, 1024), BF)] * 2 + [pltpu.VMEM((1024, 256), BF)] * 2,
        "gram", t, *parts)


def lane_bcast(x, c):
    return jnp.broadcast_to(x[:, c:c + 1], (8, 128))


def row_bcast(x, s):
    return jnp.broadcast_to(x[s:s + 1, :], (8, 128))


def total8(t):
    return ((t[0] + t[1]) + (t[2] + t[3])) + ((t[4] + t[5]) + (t[6] + t[7]))


def invert128(m, work):
    sub, lane = iotas(8, 128)
    m = list(m)
    for p in range(16):
        work(p)
        inside = (lane >= 8 * p) & (lane < 8 * p + 8)
        e = [lane_bcast(m[p], 8 * p + k) for k in range(8)]
        for s in range(0, 8, 2):
            u, v = e[s], e[s + 1]
            a, b, c, d = row_bcast(u, s), row_bcast(v, s), row_bcast(u, s + 1), row_bcast(v, s + 1)
            rd = 1.0 / (a * d - b * c)
            r0, r1 = sub == s, sub == s + 1
            new = list(e)
            for j in range(8):
                if j == s:
                    t0, t1, old = d * rd, -c * rd, 0.0
                elif j == s + 1:
                    t0, t1, old = -b * rd, a * rd, 0.0
                else:
                    x0, x1, old = row_bcast(e[j], s), row_bcast(e[j], s + 1), e[j]
                    t0, t1 = (d * x0 - b * x1) * rd, (a * x1 - c * x0) * rd
                new[j] = jnp.where(r0, t0, jnp.where(r1, t1, old - u * t0 - v * t1))
            e = new
        mp = jnp.where(inside, jnp.where(lane - 8 * p == sub, 1.0, 0.0), m[p])
        n = total8([e[k] * row_bcast(mp, k) for k in range(8)])
        nb = [row_bcast(n, k) for k in range(8)]
        for r in range(16):
            if r != p:
                t = total8([lane_bcast(m[r], 8 * p + k) * nb[k] for k in range(8)])
                m[r] = jnp.where(inside, 0.0, m[r]) - t
        m[p] = n
    return m


def solve_kern(n_parts, t_ref, g_ref, *refs):
    parts = refs[:n_parts]
    o_refs, (c_ref, x_ref, d_ref, w_ref, wh_ref, wl_ref, y_ref) = refs[n_parts:-7], refs[-7:]
    bi, bj = iotas(128, 128)
    dif = (bj - bi).astype(F32)
    eye = jnp.where(bi == bj, 1.0, 0.0)
    scale = 1.0 / (1024 * 128 * 2)
    for n, (i, j) in enumerate(OFF):
        k = g_ref[128 * n:128 * n + 128, :] * ((dif + 128.0 * (j - i)) * scale)
        c_ref[128 * i:128 * i + 128, 128 * j:128 * j + 128] = -k
        c_ref[128 * j:128 * j + 128, 128 * i:128 * i + 128] = k.T
    for m in range(4):
        k = g_ref[128 * (28 + m):128 * (29 + m), :] * (dif * scale)
        up = jnp.where(bj > bi, k, 0.0)
        low = jnp.where(bj < bi, k, 0.0)
        a = 256 * m
        c_ref[a:a + 128, a:a + 128] = eye - (up - up.T)
        c_ref[a + 128:a + 256, a + 128:a + 256] = eye - (low - low.T)
    load_pair(t_ref, parts, c_ref, 1024)
    for ref in (wh_ref, wl_ref, y_ref):
        ref[...] = jnp.zeros(ref.shape, BF)
    d_ref[...] = c_ref[0:128, 0:128]

    def update(r, cs):
        c_ref[r, cs] = c_ref[r, cs] - (dot(y_ref[r, :], wh_ref[:, cs]) + dot(y_ref[r, :], wl_ref[:, cs]))

    def work(p):
        update(slice(256 * (p // 4) + 256, 256 * (p // 4) + 512), slice(256 * (p % 4), 256 * (p % 4) + 256))

    def step(k, _):
        kc = pl.ds(pl.multiple_of(k * 128, 128), 128)
        m = invert128([d_ref[8 * r:8 * r + 8, :] for r in range(16)], work)
        for r in range(16):
            d_ref[8 * r:8 * r + 8, :] = m[r]
        c_ref[kc, kc] = jnp.zeros((128, 128), F32)
        dh, dl = split(d_ref[...])
        w_ref[0:128, 0:128] = dh
        w_ref[128:256, 0:128] = dh
        w_ref[0:128, 128:256] = dl
        w_ref[128:256, 128:256] = dl
        for c in range(0, 1024, 256):
            hi, lo = split(c_ref[kc, c:c + 256])
            wh_ref[0:128, c:c + 256] = hi
            wh_ref[128:256, c:c + 256] = hi
            wl_ref[0:128, c:c + 256] = lo
            wl_ref[128:256, c:c + 256] = lo

        def rows(i, _):
            r = pl.ds(pl.multiple_of(i * 256, 256), 256)
            y = dot(jnp.concatenate(split(c_ref[r, kc]), axis=1), w_ref[...])
            y = y[:, :128] + y[:, 128:]
            y_ref[r, :] = jnp.concatenate(split(y), axis=1)
            c_ref[r, kc] = y
            return 0

        lax.fori_loop((k + 1) // 2, 5, rows, 0)

        def first_rows(i, _):
            for c in range(0, 1024, 256):
                update(slice(0, 256), slice(c, c + 256))
            return 0

        lax.fori_loop(k, 1, first_rows, 0)
        nc = pl.ds(pl.multiple_of(jnp.minimum(k + 1, 7) * 128, 128), 128)
        gone = jnp.where(k == 0, 0.0, 1.0)
        y = y_ref[nc, :]
        d_ref[...] = c_ref[nc, nc] - gone * (dot(y, wh_ref[:, nc]) + dot(y, wl_ref[:, nc]))
        return 0

    lax.fori_loop(0, 8, step, 0)
    load_pair(t_ref, parts, x_ref, 0)
    for c in range(0, 1024, 256):
        update(slice(1024, 1280), slice(c, c + 256))
    if n_parts == 1:
        for o_ref, half in zip(o_refs, (t_ref[5], 1 - t_ref[5])):
            cs = pl.ds(pl.multiple_of(half * 512, 512), 512)
            o_ref[...] = 2.0 * c_ref[1024:1280, cs] - x_ref[:, cs]
    else:
        for n in range(2):
            cs = slice(512 * n, 512 * n + 512)
            o_refs[0][n] = 2.0 * c_ref[1024:1280, cs] - x_ref[:, cs]


def solve(t, g, parts):
    half = jax.ShapeDtypeStruct((256, 512), F32)
    return vmem_call(
        functools.partial(solve_kern, len(parts)),
        (half, half) if len(parts) == 1 else jax.ShapeDtypeStruct((2, 256, 512), F32),
        1,
        [pltpu.VMEM((1280, 1024), F32), pltpu.VMEM((256, 1024), F32), pltpu.VMEM((128, 128), F32),
         pltpu.VMEM((256, 256), BF)] + [pltpu.VMEM((256, 1024), BF)] * 2 + [pltpu.VMEM((1280, 256), BF)],
        "solve", t, g, *parts)


def comm_kern(g_ref, o_ref, r1, h, r2a, r2b, qa, qb, r3a, r3b, *sems):
    row = lax.axis_index("row")
    c = lax.rem(row, 2)
    y = lax.rem(row // 2, NY)
    z = row // (2 * NY)
    ys = [lax.rem(y + d, NY) for d in range(NY)]
    zs = [lax.rem(z + d, NZ) for d in range(NZ)]
    ydev = [{"row": (z * NY + ys[d]) * 2 + c} for d in range(NY)]
    zdev = [{"row": (zs[d] * NY + y) * 2 + c} for d in range(NZ)]
    other = {"row": (z * NY + y) * 2 + 1 - c}
    half = c * HALF

    def at(start, size):
        return pl.ds(pl.multiple_of(start, 8), size)

    barrier = pltpu.get_barrier_semaphore()
    for target in [other] + ydev[1:] + zdev[1:]:
        pl.semaphore_signal(barrier, inc=1, device_id=target, device_id_type=MESH)
    pl.semaphore_wait(barrier, NY + NZ - 1)

    sent = []

    def send(src, dst, pair, n, target):
        copy = pltpu.make_async_remote_copy(
            src_ref=src, dst_ref=dst, send_sem=sems[2 * pair].at[n], recv_sem=sems[2 * pair + 1].at[n],
            device_id=target, device_id_type=MESH)
        copy.start()
        sent.append(copy)
        return copy

    chunks = [at(ys[d] * YA, YA) for d in (1, 3, 2)] + [at(PA, PB), at(y * YA, YA)]
    core = [send(g_ref.at[at((1 - c) * HALF + s.start, s.size)], r1.at[s], 0, n, other) for n, s in enumerate(chunks)]

    def add(s):
        h[s, :] = g_ref[at(half + s.start, s.size), :] + r1[s, :]

    sums_ya, sums_zb = [], []
    for n, d in enumerate((1, 3, 2)):
        core[n].wait_recv()
        add(chunks[n])
        sums_ya.append(send(h.at[chunks[n]], r2a.at[d - 1], 1, d - 1, ydev[d]))
    core[3].wait_recv()
    for d in ZORDER:
        s = at(PA + zs[d] * ZB, ZB)
        add(s)
        sums_zb.append(send(h.at[s], r2b.at[d - 1], 2, d - 1, zdev[d]))
    add(at(PA + z * ZB, ZB))
    core[4].wait_recv()
    add(chunks[4])

    for copy in sums_zb:
        copy.wait_recv()
    total = h[at(PA + z * ZB, ZB), :]
    for d in range(NZ - 1):
        total = total + r2b[d]
    qb[...] = total
    sums_yb = [send(qb.at[at(ys[d] * YB, YB)], r3b.at[d - 1], 3, d - 1, ydev[d]) for d in (2, 1, 3)]

    for copy in sums_ya:
        copy.wait_recv()
    sums_za = []
    for d in ZORDER + (0,):
        s = at(zs[d] * ZA, ZA)
        qa[s, :] = (h[at(y * YA + zs[d] * ZA, ZA), :] + r2a[0, s, :]) + (r2a[1, s, :] + r2a[2, s, :])
        if d:
            sums_za.append(send(qa.at[s], r3a.at[d - 1], 4, d - 1, zdev[d]))

    for copy in sums_yb:
        copy.wait_recv()
    mine = at(half + PA + z * ZB + y * YB, YB)
    o_ref[mine, :] = (qb[at(y * YB, YB), :] + r3b[0]) + (r3b[1] + r3b[2])
    back_yb = [send(o_ref.at[mine], o_ref.at[mine], 5, d - 1, ydev[d]) for d in (2, 1, 3)]

    for copy in sums_za:
        copy.wait_recv()
    total = qa[at(z * ZA, ZA), :]
    for d in range(NZ - 1):
        total = total + r3a[d]
    mine = at(half + y * YA + z * ZA, ZA)
    o_ref[mine, :] = total
    back_za = [send(o_ref.at[mine], o_ref.at[mine], 6, d - 1, zdev[d]) for d in ZORDER]

    for copy in back_yb:
        copy.wait_recv()
    own = at(half + PA + z * ZB, ZB)
    back_zb = [send(o_ref.at[own], o_ref.at[own], 7, d - 1, zdev[d]) for d in ZORDER]
    for copy in back_za:
        copy.wait_recv()
    own = at(half + y * YA, YA)
    back_ya = [send(o_ref.at[own], o_ref.at[own], 8, d - 1, ydev[d]) for d in (2, 1, 3)]
    back = [send(o_ref.at[own], o_ref.at[own], 9, 0, other)]
    for copy in back_zb:
        copy.wait_recv()
    part = at(half + PA, PB)
    back.append(send(o_ref.at[part], o_ref.at[part], 9, 1, other))
    for n, d in enumerate((2, 1, 3)):
        back_ya[n].wait_recv()
        part = at(half + lax.rem(y + NY - d, NY) * YA, YA)
        back.append(send(o_ref.at[part], o_ref.at[part], 9, 2 + n, other))
    for copy in back:
        copy.wait_recv()
    for copy in sent:
        copy.wait_send()


def comm(g):
    counts = (5, 3, 7, 3, 7, 3, 7, 7, 3, 5)
    buffers = ((HALF,), (HALF,), (3, YA), (7, ZB), (YA,), (ZB,), (7, ZA), (3, YB))
    return pl.pallas_call(
        comm_kern,
        out_shape=jax.ShapeDtypeStruct((2 * HALF, 128), F32),
        in_specs=[pl.BlockSpec(memory_space=pltpu.VMEM)],
        out_specs=pl.BlockSpec(memory_space=pltpu.VMEM),
        scratch_shapes=[pltpu.VMEM(b + (128,), F32) for b in buffers]
        + [pltpu.SemaphoreType.DMA((n,)) for n in counts for _ in range(2)],
        compiler_params=pltpu.CompilerParams(
            vmem_limit_bytes=24 * 2**20, collective_id=0, has_side_effects=True),
        name="comm")(g)


def swap_kern(n_blocks, t_ref, x_ref, o_ref, mid, out, ss1, rs1, ss2, rs2):
    me = lax.axis_index("pair")
    others = [lax.rem(me + d, 4) for d in range(4)]
    barrier = pltpu.get_barrier_semaphore()
    for d in (2, 1, 3):
        pl.semaphore_signal(barrier, inc=1, device_id={"pair": others[d]}, device_id_type=MESH)
    pl.semaphore_wait(barrier, 3)

    def rows(j):
        return pl.ds(pl.multiple_of(64 * j, 64), 64)

    def send(src, dst, ss, rs, d):
        copy = pltpu.make_async_remote_copy(
            src_ref=src, dst_ref=dst, send_sem=ss.at[d - 1], recv_sem=rs.at[d - 1],
            device_id={"pair": others[d]}, device_id_type=MESH)
        copy.start()
        return copy

    there = [send(x_ref.at[:, rows(others[d]), :], mid.at[:, me], ss1, rs1, d) for d in (2, 1, 3)]
    mid[:, me] = x_ref[:, rows(me), :]
    for copy in there:
        copy.wait_recv()
    back = []
    for d in (2, 1, 3, 0):
        for n in range(n_blocks):
            at = t_ref[8 + n_blocks * others[d] + n] if n_blocks == 2 else t_ref[others[d]]
            block = mid[at // 4, at % 4]
            if d:
                out[d - 1, :, 512 * n:512 * n + 512] = block
            else:
                o_ref[rows(me), 512 * n:512 * n + 512] = block
        if d:
            back.append(send(out.at[d - 1], o_ref.at[rows(me), :], ss2, rs2, d))
    for copy in back:
        copy.wait_recv()
    for copy in there + back:
        copy.wait_send()


def swap(t, x):
    n = x.shape[0]
    vm = pl.BlockSpec(memory_space=pltpu.VMEM)
    return pl.pallas_call(
        functools.partial(swap_kern, n),
        out_shape=jax.ShapeDtypeStruct((256, 512 * n), F32),
        in_specs=[pl.BlockSpec(memory_space=pltpu.SMEM), vm],
        out_specs=vm,
        scratch_shapes=[pltpu.VMEM((n, 4, 64, 512), F32), pltpu.VMEM((3, 64, 512 * n), F32)]
        + [pltpu.SemaphoreType.DMA((3,))] * 4,
        compiler_params=pltpu.CompilerParams(
            vmem_limit_bytes=16 * 2**20, collective_id=n, has_side_effects=True),
        name="swap")(t, x)


def route_kern(plan_ref, t_ref):
    me = lax.axis_index("pair")

    def pick(values, n):
        out = values[0]
        for i in range(1, len(values)):
            out = jnp.where(n == i, values[i], out)
        return out

    def place(values, v):
        return sum(i * (x == v).astype(jnp.int32) for i, x in enumerate(values))

    first = [plan_ref[0, 2 * q] for q in range(4)]
    second = [plan_ref[0, 2 * q + 1] for q in range(4)]
    one = [jnp.left_shift(1, v >> 1) for v in first]
    two = [jnp.left_shift(1, v >> 1) for v in second]
    best = jnp.int32(0)
    for mask in range(16):
        seen = 0
        for q in range(4):
            seen = seen | (two[q] if mask >> q & 1 else one[q])
        best = jnp.where(seen == 15, mask, best)
    bit = [jnp.right_shift(best, q) & 1 for q in range(4)]
    kept = [jnp.where(bit[q] == 1, second[q], first[q]) for q in range(4)]
    moved = [jnp.where(bit[q] == 1, first[q], second[q]) for q in range(4)]
    home = [v >> 1 for v in kept]
    for d in range(4):
        t_ref[d] = pick(moved, place(home, d)) >> 1
    mine = place(home, me)
    t_ref[4] = pick(bit, mine)
    t_ref[5] = pick(kept, mine) & 1
    t_ref[6] = 0
    t_ref[7] = 0
    where = [4 * (i % 2) + home[i // 2] for i in range(8)]
    blocks = [plan_ref[0, i] for i in range(8)]
    for p in range(8):
        t_ref[8 + p] = pick(where, place(blocks, plan_ref[1, p]))


def route(plan):
    return pl.pallas_call(
        route_kern,
        out_shape=jax.ShapeDtypeStruct((16,), jnp.int32),
        in_specs=[pl.BlockSpec(memory_space=pltpu.SMEM)],
        out_specs=pl.BlockSpec(memory_space=pltpu.SMEM),
        name="route")(plan)


def body(matrix, plan):
    t = route(plan)
    keep, away = solve(t, comm(gram(t, (matrix,))), (matrix,))
    parts = (keep, swap(t, away[None]))
    return swap(t, solve(t, comm(gram(t, parts)), parts))


def solution(mesh):
    placed = (P("row", "pair"), P())
    return jax.shard_map(
        body, mesh=mesh, in_specs=placed, out_specs=P("row", "pair"), check_vma=False
    )
```

profile of v0, /device:TPU:1, one launch (start us, length us, event | category | flops | bytes accessed | tf_op | source)
XLA Modules:
  0.0 237.3 jit_solution(5252661022982067096)
XLA Ops:
  0.0 1.4 route.1.t_ref
  1.4 0.0 copy-start
  1.4 1.2 copy-done
  2.6 0.0 copy-start.1
  2.6 0.7 copy-done.1
  3.3 1.8 gram.2.g_ref
  5.1 45.8 %comm.2.g_ref = f32[4096,128]{1,0:T(8,128)S(1)} custom-call(f32[4096,128]{1,0:T(8,128)S(1)} %gram.2.g_ref), custom_call_target="tpu_custom_call" | custom-call | tf_op jit(solution)/shard_map/comm/pallas_call | solution.py:339
  50.9 46.2 %solve.2 = (f32[256,512]{1,0:T(8,128)S(1)}, f32[256,512]{1,0:T(8,128)S(1)}) custom-call(s32[16]{0:T(128)S(1)} %copy-done.1, f32[4096,128]{1,0:T(8,128)S(1)} %comm.2.g_ref, f32[256,1024]{1,0:T(8,128)S(1)} %copy-done), custom_call_target="tpu_custom_call" | custom-call | tf_op jit(solution)/shard_map/solve/pallas_call | solution.py:38
  97.1 19.7 %swap.2.refs_1_ = f32[256,512]{1,0:T(8,128)S(1)} custom-call(s32[16]{0:T(128)S(1)} %copy-done.1, f32[1,256,512]{2,1,0:T(8,128)S(1)} %bitcast.1), custom_call_target="tpu_custom_call" | custom-call | tf_op jit(solution)/shard_map/swap/pallas_call | solution.py:393
  116.8 1.8 gram.3.g_ref
  118.7 41.4 %comm.3.g_ref = f32[4096,128]{1,0:T(8,128)S(1)} custom-call(f32[4096,128]{1,0:T(8,128)S(1)} %gram.3.g_ref), custom_call_target="tpu_custom_call" | custom-call | tf_op jit(solution)/shard_map/comm/pallas_call | solution.py:339
  160.1 46.3 %solve.3.x_ref = f32[2,256,512]{2,1,0:T(8,128)S(1)} custom-call(s32[16]{0:T(128)S(1)} %copy-done.1, f32[4096,128]{1,0:T(8,128)S(1)} %comm.3.g_ref, f32[256,512]{1,0:T(8,128)S(1)} %get-tuple-element.7.refs_0_, f32[256,512]{1,0:T(8,128)S(1)} %swap.2.refs_1_), custom_call_target="tpu_custom_call" | custom-call | tf_op jit(solution)/shard_map/solve/pallas_call | solution.py:38
  206.4 30.0 %swap.3 = f32[256,1024]{1,0:T(8,128)S(1)} custom-call(s32[16]{0:T(128)S(1)} %copy-done.1, f32[2,256,512]{2,1,0:T(8,128)S(1)} %solve.3.x_ref), custom_call_target="tpu_custom_call" | custom-call | tf_op jit(solution)/shard_map/swap/pallas_call | solution.py:393
  236.3 1.0 copy.4
Async XLA Ops:
  1.4 1.2 copy-start
  2.6 0.7 copy-start.1
where the time goes:
time: 237 us
  Pallas kernels  234 us (99%)
  local copies, waits for them, and re-layouts  2.85 us (1%)
    pallas_call x4, Pallas kernels, vmem_call(): pl.pallas_call(kern, out_shape=outs, in_specs=[sm] * n_smem + [vm] * (len...  96.1 us
    pallas_call x2, Pallas kernels, comm(): pl.pallas_call(comm_kern, out_shape=jax.ShapeDtypeStruct((2 * HALF, 128),...  87.2 us
    pallas_call x2, Pallas kernels, swap(): pl.pallas_call(functools.partial(swap_kern, n), out_shape=jax.ShapeDtypeS...  49.7 us

commit v1 on v0

--- a/solution.py
+++ b/solution.py
@@ -13,7 +13,7 @@
 MESH = pl.DeviceIdType.MESH
 OFF = [(i, j) for i in range(8) for j in range(i + 1, 8)]
 NZ, NY = 8, 4
-HALF, PA, PB = 2048, 1536, 512
+HALF, PA, PB = 2048, 1280, 768
 YA, ZA, ZB, YB = PA // NY, PA // NY // NZ, PB // NZ, PB // NZ // NY
 ZORDER = (4, 3, 5, 2, 6, 1, 7)
 
@@ -39,7 +39,7 @@
         kern,
         out_shape=outs,
         in_specs=[sm] * n_smem + [vm] * (len(args) - n_smem),
-        out_specs=jax.tree.map(lambda _: vm, outs),
+        out_specs=jax.tree.map(lambda out: sm if out.dtype == jnp.int32 else vm, outs),
         scratch_shapes=scratch,
         compiler_params=pltpu.CompilerParams(vmem_limit_bytes=32 * 2**20),
         name=name,
@@ -57,7 +57,11 @@
 
 def gram_kern(n_parts, t_ref, *refs):
     parts = refs[:n_parts]
-    g_ref, x_ref, ph, plo, th, tl = refs[n_parts:]
+    if n_parts == 1:
+        g_ref, table_ref, x_ref, ph, plo, th, tl = refs[n_parts:]
+        route(t_ref, table_ref)
+    else:
+        g_ref, x_ref, ph, plo, th, tl = refs[n_parts:]
     load_pair(t_ref, parts, x_ref, 0)
     for c in range(0, 1024, 256):
         x = x_ref[:, c:c + 256]
@@ -80,9 +84,10 @@
 
 
 def gram(t, parts):
+    out = jax.ShapeDtypeStruct((4096, 128), F32)
     return vmem_call(
         functools.partial(gram_kern, len(parts)),
-        jax.ShapeDtypeStruct((4096, 128), F32),
+        (out, jax.ShapeDtypeStruct((16,), jnp.int32)) if len(parts) == 1 else out,
         1,
         [pltpu.VMEM((256, 1024), F32)] + [pltpu.VMEM((256, 1024), BF)] * 2 + [pltpu.VMEM((1024, 256), BF)] * 2,
         "gram", t, *parts)
@@ -100,43 +105,64 @@
     return ((t[0] + t[1]) + (t[2] + t[3])) + ((t[4] + t[5]) + (t[6] + t[7]))
 
 
+def panel_product(m, n, p):
+    x0, x1 = split(jnp.concatenate(m, axis=0))
+    zero = [jnp.zeros((8, 128), F32)]
+    y0, y1 = split(jnp.concatenate(zero * p + [n] + zero * (15 - p), axis=0))
+    top = jnp.concatenate([y0, y1], axis=1)
+    u = dot(jnp.concatenate([x0, x1], axis=1), jnp.concatenate([top, top], axis=0))
+    return u[:, :128] + u[:, 128:]
+
+
 def invert128(m, work):
     sub, lane = iotas(8, 128)
     m = list(m)
+    e = [lane_bcast(m[0], k) for k in range(8)]
     for p in range(16):
+        nxt = (p + 1) % 16
+        left = [lane_bcast(m[nxt], 8 * p + k) for k in range(8)]
         work(p)
+        upper = [lane_bcast(m[p], 8 * p + 8 + k) for k in range(8 if p < 15 else 0)]
+        corner = [lane_bcast(m[nxt], 8 * p + 8 + k) for k in range(8 if p < 15 else 0)]
+        after = (p + 2) % 16
+        left2 = [lane_bcast(m[after], 8 * p + k) for k in range(8)]
         inside = (lane >= 8 * p) & (lane < 8 * p + 8)
-        e = [lane_bcast(m[p], 8 * p + k) for k in range(8)]
         for s in range(0, 8, 2):
             u, v = e[s], e[s + 1]
             a, b, c, d = row_bcast(u, s), row_bcast(v, s), row_bcast(u, s + 1), row_bcast(v, s + 1)
             rd = 1.0 / (a * d - b * c)
+            a, b, c, d = a * rd, b * rd, c * rd, d * rd
             r0, r1 = sub == s, sub == s + 1
+            both = (sub >= s) & (sub <= s + 1)
+            u, v = jnp.where(both, jnp.where(r0, -1.0, 0.0), u), jnp.where(both, jnp.where(r1, -1.0, 0.0), v)
             new = list(e)
             for j in range(8):
                 if j == s:
-                    t0, t1, old = d * rd, -c * rd, 0.0
+                    new[j] = v * c - u * d
                 elif j == s + 1:
-                    t0, t1, old = -b * rd, a * rd, 0.0
+                    new[j] = u * b - v * a
                 else:
-                    x0, x1, old = row_bcast(e[j], s), row_bcast(e[j], s + 1), e[j]
-                    t0, t1 = (d * x0 - b * x1) * rd, (a * x1 - c * x0) * rd
-                new[j] = jnp.where(r0, t0, jnp.where(r1, t1, old - u * t0 - v * t1))
+                    x0, x1 = row_bcast(e[j], s), row_bcast(e[j], s + 1)
+                    new[j] = jnp.where(both, 0.0, e[j]) - u * (d * x0 - b * x1) - v * (a * x1 - c * x0)
             e = new
+        ahead = []
+        for k in range(len(corner)):
+            x = total8([e[i] * row_bcast(upper[k], i) for i in range(8)])
+            ahead.append(corner[k] - total8([left[i] * row_bcast(x, i) for i in range(8)]))
         mp = jnp.where(inside, jnp.where(lane - 8 * p == sub, 1.0, 0.0), m[p])
         n = total8([e[k] * row_bcast(mp, k) for k in range(8)])
-        nb = [row_bcast(n, k) for k in range(8)]
+        soon = jnp.where(inside, 0.0, m[nxt]) - total8([left[k] * row_bcast(n, k) for k in range(8)])
+        soon2 = jnp.where(inside, 0.0, m[after]) - total8([left2[k] * row_bcast(n, k) for k in range(8)])
+        e = ahead
+        t = panel_product(m, n, p)
         for r in range(16):
-            if r != p:
-                t = total8([lane_bcast(m[r], 8 * p + k) * nb[k] for k in range(8)])
-                m[r] = jnp.where(inside, 0.0, m[r]) - t
-        m[p] = n
+            m[r] = n if r == p else soon if r == nxt else soon2 if r == after else jnp.where(inside, 0.0, m[r]) - t[8 * r:8 * r + 8, :]
     return m
 
 
 def solve_kern(n_parts, t_ref, g_ref, *refs):
     parts = refs[:n_parts]
-    o_refs, (c_ref, x_ref, d_ref, w_ref, wh_ref, wl_ref, y_ref) = refs[n_parts:-7], refs[-7:]
+    o_refs, (c_ref, x_ref, d_ref, w_ref, a_ref, y_ref) = refs[n_parts:-6], refs[-6:]
     bi, bj = iotas(128, 128)
     dif = (bj - bi).astype(F32)
     eye = jnp.where(bi == bj, 1.0, 0.0)
@@ -153,60 +179,79 @@
         c_ref[a:a + 128, a:a + 128] = eye - (up - up.T)
         c_ref[a + 128:a + 256, a + 128:a + 256] = eye - (low - low.T)
     load_pair(t_ref, parts, c_ref, 1024)
-    for ref in (wh_ref, wl_ref, y_ref):
+    for ref in (w_ref, y_ref):
         ref[...] = jnp.zeros(ref.shape, BF)
     d_ref[...] = c_ref[0:128, 0:128]
 
+    def columns(k):
+        return pl.ds(pl.multiple_of(k * 128, 128), 128)
+
+    def scaled(r, kc):
+        y = dot(jnp.concatenate(split(c_ref[r, kc]), axis=1), w_ref[...])
+        y = y[:, :128] + y[:, 128:]
+        return y, jnp.concatenate(split(y) * 2, axis=1)
+
+    def pivot_rows(kc, cs):
+        hi, lo = split(c_ref[kc, cs])
+        for i, x in enumerate((hi, hi, lo, lo)):
+            a_ref[128 * i:128 * i + 128, cs] = x
+
     def update(r, cs):
-        c_ref[r, cs] = c_ref[r, cs] - (dot(y_ref[r, :], wh_ref[:, cs]) + dot(y_ref[r, :], wl_ref[:, cs]))
-
-    def work(p):
-        update(slice(256 * (p // 4) + 256, 256 * (p // 4) + 512), slice(256 * (p % 4), 256 * (p % 4) + 256))
-
-    def step(k, _):
-        kc = pl.ds(pl.multiple_of(k * 128, 128), 128)
+        c_ref[r, cs] = c_ref[r, cs] - dot(y_ref[r, :], a_ref[:, cs])
+
+    def step(first, k, _):
+        before = columns(jnp.maximum(k - 1, 0))
+
+        def work(p):
+            each = 4 * (5 - first)
+            if p * each % 16 >= each:
+                return
+            p = p * each // 16
+            r = slice(256 * (p // 4 + first), 256 * (p // 4 + first) + 256)
+            cs = slice(256 * (p % 4), 256 * (p % 4) + 256)
+            if p < 4:
+                pivot_rows(before, cs)
+            if p % 4 == 0:
+                y, y_ref[r, :] = scaled(r, before)
+                c_ref[r, before] = jnp.where(k == 0, c_ref[r, before], y)
+            update(r, cs)
+
         m = invert128([d_ref[8 * r:8 * r + 8, :] for r in range(16)], work)
         for r in range(16):
             d_ref[8 * r:8 * r + 8, :] = m[r]
+        kc = columns(k)
         c_ref[kc, kc] = jnp.zeros((128, 128), F32)
         dh, dl = split(d_ref[...])
         w_ref[0:128, 0:128] = dh
         w_ref[128:256, 0:128] = dh
         w_ref[0:128, 128:256] = dl
         w_ref[128:256, 128:256] = dl
-        for c in range(0, 1024, 256):
-            hi, lo = split(c_ref[kc, c:c + 256])
-            wh_ref[0:128, c:c + 256] = hi
-            wh_ref[128:256, c:c + 256] = hi
-            wl_ref[0:128, c:c + 256] = lo
-            wl_ref[128:256, c:c + 256] = lo
-
-        def rows(i, _):
-            r = pl.ds(pl.multiple_of(i * 256, 256), 256)
-            y = dot(jnp.concatenate(split(c_ref[r, kc]), axis=1), w_ref[...])
-            y = y[:, :128] + y[:, 128:]
-            y_ref[r, :] = jnp.concatenate(split(y), axis=1)
+        nc = columns(jnp.minimum(k + 1, 7))
+        hi, lo = split(c_ref[kc, nc])
+        _, y = scaled(nc, kc)
+        d_ref[...] = c_ref[nc, nc] - dot(y, jnp.concatenate([hi, hi, lo, lo], axis=0))
+
+        def first_rows(i, _):
+            r = slice(0, 256)
+            y, y_ref[r, :] = scaled(r, kc)
             c_ref[r, kc] = y
+            for c in range(0, 1024, 256):
+                pivot_rows(kc, slice(c, c + 256))
+                update(r, slice(c, c + 256))
             return 0
 
-        lax.fori_loop((k + 1) // 2, 5, rows, 0)
-
-        def first_rows(i, _):
-            for c in range(0, 1024, 256):
-                update(slice(0, 256), slice(c, c + 256))
-            return 0
-
         lax.fori_loop(k, 1, first_rows, 0)
-        nc = pl.ds(pl.multiple_of(jnp.minimum(k + 1, 7) * 128, 128), 128)
-        gone = jnp.where(k == 0, 0.0, 1.0)
-        y = y_ref[nc, :]
-        d_ref[...] = c_ref[nc, nc] - gone * (dot(y, wh_ref[:, nc]) + dot(y, wl_ref[:, nc]))
         return 0
 
-    lax.fori_loop(0, 8, step, 0)
+    for first, start, stop in ((1, 0, 4), (2, 4, 6), (3, 6, 8)):
+        lax.fori_loop(start, stop, functools.partial(step, first), 0)
+    last = slice(896, 1024)
+    y, y_ref[1024:1280, :] = scaled(slice(1024, 1280), last)
+    c_ref[1024:1280, last] = y
+    for c in range(0, 1024, 256):
+        pivot_rows(last, slice(c, c + 256))
+        update(slice(1024, 1280), slice(c, c + 256))
     load_pair(t_ref, parts, x_ref, 0)
-    for c in range(0, 1024, 256):
-        update(slice(1024, 1280), slice(c, c + 256))
     if n_parts == 1:
         for o_ref, half in zip(o_refs, (t_ref[5], 1 - t_ref[5])):
             cs = pl.ds(pl.multiple_of(half * 512, 512), 512)
@@ -224,7 +269,7 @@
         (half, half) if len(parts) == 1 else jax.ShapeDtypeStruct((2, 256, 512), F32),
         1,
         [pltpu.VMEM((1280, 1024), F32), pltpu.VMEM((256, 1024), F32), pltpu.VMEM((128, 128), F32),
-         pltpu.VMEM((256, 256), BF)] + [pltpu.VMEM((256, 1024), BF)] * 2 + [pltpu.VMEM((1280, 256), BF)],
+         pltpu.VMEM((256, 256), BF)] + [pltpu.VMEM((512, 1024), BF), pltpu.VMEM((1280, 512), BF)],
         "solve", t, g, *parts)
 
 
@@ -402,7 +447,7 @@
         name="swap")(t, x)
 
 
-def route_kern(plan_ref, t_ref):
+def route(plan_ref, t_ref):
     me = lax.axis_index("pair")
 
     def pick(values, n):
@@ -441,18 +486,9 @@
         t_ref[8 + p] = pick(where, place(blocks, plan_ref[1, p]))
 
 
-def route(plan):
-    return pl.pallas_call(
-        route_kern,
-        out_shape=jax.ShapeDtypeStruct((16,), jnp.int32),
-        in_specs=[pl.BlockSpec(memory_space=pltpu.SMEM)],
-        out_specs=pl.BlockSpec(memory_space=pltpu.SMEM),
-        name="route")(plan)
-
-
 def body(matrix, plan):
-    t = route(plan)
-    keep, away = solve(t, comm(gram(t, (matrix,))), (matrix,))
+    g, t = gram(plan, (matrix,))
+    keep, away = solve(t, comm(g), (matrix,))
     parts = (keep, swap(t, away[None]))
     return swap(t, solve(t, comm(gram(t, parts)), parts))
 

time: 237 us -> 217 us (0.916)
  Pallas kernels: 234 us -> 214 us
    pallas_call x4, Pallas kernels: 96.1 us -> 79.8 us  [vmem_call(): pl.pallas_call(kern, out_shape=outs, in_specs=[sm] * n_smem + [vm] * (len...]
where the time goes in v1:
time: 217 us
  Pallas kernels  214 us (99%)
  local copies, waits for them, and re-layouts  2.88 us (1%)
    pallas_call x2, Pallas kernels, comm(): pl.pallas_call(comm_kern, out_shape=jax.ShapeDtypeStruct((2 * HALF, 128),...  86.3 us
    pallas_call x4, Pallas kernels, vmem_call(): pl.pallas_call(kern, out_shape=outs, in_specs=[sm] * n_smem + [vm] * (len...  79.8 us
    pallas_call x2, Pallas kernels, swap(): pl.pallas_call(functools.partial(swap_kern, n), out_shape=jax.ShapeDtypeS...  48.2 us

profile of v1, /device:TPU:1, one launch (start us, length us, event | category | flops | bytes accessed | tf_op | source)
XLA Modules:
  0.0 217.2 jit_solution(7055231990120747132)
XLA Ops:
  0.0 0.0 copy-start
  0.0 1.2 copy-done
  1.2 0.0 copy-start.2
  1.2 0.7 copy-done.2
  1.9 2.5 %gram.2 = (f32[4096,128]{1,0:T(8,128)S(1)}, s32[16]{0:T(128)S(1)}) custom-call(s32[2,8]{1,0:T(2,128)S(1)} %copy-done.2, f32[256,1024]{1,0:T(8,128)S(1)} %copy-done), custom_call_target="tpu_custom_call" | custom-call | tf_op jit(solution)/shard_map/gram/pallas_call | solution.py:38
  4.4 0.0 copy-start.1
  4.4 45.6 %comm.2.g_ref = f32[4096,128]{1,0:T(8,128)S(1)} custom-call(f32[4096,128]{1,0:T(8,128)S(1)} %get-tuple-element.10.g_ref), custom_call_target="tpu_custom_call" | custom-call | tf_op jit(solution)/shard_map/comm/pallas_call | solution.py:384
  50.0 0.0 copy-done.1
  50.0 37.6 %solve.2 = (f32[256,512]{1,0:T(8,128)S(1)}, f32[256,512]{1,0:T(8,128)S(1)}) custom-call(s32[16]{0:T(128)S(1)} %get-tuple-element.9.t_ref, f32[4096,128]{1,0:T(8,128)S(1)} %comm.2.g_ref, f32[256,1024]{1,0:T(8,128)S(1)} %copy-done.1), custom_call_target="tpu_custom_call" | custom-call | tf_op jit(solution)/shard_map/solve/pallas_call | solution.py:38
  87.6 18.9 %swap.2.refs_1_ = f32[256,512]{1,0:T(8,128)S(1)} custom-call(s32[16]{0:T(128)S(1)} %get-tuple-element.9.t_ref, f32[1,256,512]{2,1,0:T(8,128)S(1)} %bitcast.1), custom_call_target="tpu_custom_call" | custom-call | tf_op jit(solution)/shard_map/swap/pallas_call | solution.py:438
  106.5 1.8 gram.3.g_ref
  108.4 40.7 %comm.3.g_ref = f32[4096,128]{1,0:T(8,128)S(1)} custom-call(f32[4096,128]{1,0:T(8,128)S(1)} %gram.3.g_ref), custom_call_target="tpu_custom_call" | custom-call | tf_op jit(solution)/shard_map/comm/pallas_call | solution.py:384
  149.1 37.9 %solve.3.x_ref = f32[2,256,512]{2,1,0:T(8,128)S(1)} custom-call(s32[16]{0:T(128)S(1)} %get-tuple-element.9.t_ref, f32[4096,128]{1,0:T(8,128)S(1)} %comm.3.g_ref, f32[256,512]{1,0:T(8,128)S(1)} %get-tuple-element.11.refs_0_, f32[256,512]{1,0:T(8,128)S(1)} %swap.2.refs_1_), custom_call_target="tpu_custom_call" | custom-call | tf_op jit(solution)/shard_map/solve/pallas_call | solution.py:38
  187.0 29.2 %swap.3 = f32[256,1024]{1,0:T(8,128)S(1)} custom-call(s32[16]{0:T(128)S(1)} %get-tuple-element.9.t_ref, f32[2,256,512]{2,1,0:T(8,128)S(1)} %solve.3.x_ref), custom_call_target="tpu_custom_call" | custom-call | tf_op jit(solution)/shard_map/swap/pallas_call | solution.py:438
  216.3 1.0 copy.4
Async XLA Ops:
  0.0 1.2 copy-start
  1.2 0.7 copy-start.2
  4.4 45.6 %copy-start.1 = (f32[256,1024]{1,0:T(8,128)S(1)}, f32[256,1024]{1,0:T(8,128)}, u32[]{:S(2)}) copy-start(f32[256,1024]{1,0:T(8,128)} %refs_0_.3) | copy-start | bytes 3145732

commit v2 on v1

--- a/solution.py
+++ b/solution.py
@@ -13,9 +13,11 @@
 MESH = pl.DeviceIdType.MESH
 OFF = [(i, j) for i in range(8) for j in range(i + 1, 8)]
 NZ, NY = 8, 4
-HALF, PA, PB = 2048, 1280, 768
+NA, HALF, PA, PB = 2, 2048, 768, 512
 YA, ZA, ZB, YB = PA // NY, PA // NY // NZ, PB // NZ, PB // NZ // NY
+YORDER = (2, 1, 3)
 ZORDER = (4, 3, 5, 2, 6, 1, 7)
+NS = 2
 
 
 def split(x):
@@ -273,7 +275,9 @@
         "solve", t, g, *parts)
 
 
-def comm_kern(g_ref, o_ref, r1, h, r2a, r2b, qa, qb, r3a, r3b, *sems):
+def comm_kern(g_ref, o_ref, r1, h, qa, qb, *rest):
+    r2a, r3a, r2b, r3b = rest[:NA], rest[NA:2 * NA], rest[2 * NA], rest[2 * NA + 1]
+    sems = rest[2 * NA + 2:]
     row = lax.axis_index("row")
     c = lax.rem(row, 2)
     y = lax.rem(row // 2, NY)
@@ -303,84 +307,104 @@
         sent.append(copy)
         return copy
 
-    chunks = [at(ys[d] * YA, YA) for d in (1, 3, 2)] + [at(PA, PB), at(y * YA, YA)]
+    def came(copies):
+        for copy in copies:
+            copy.wait_recv()
+
+    ya = [[at(PA * i + ys[d] * YA, YA) for d in range(NY)] for i in range(NA)]
+    chunks = [ya[0][d] for d in YORDER] + [at(NA * PA, PB), ya[0][0]]
+    chunks += [ya[i][d] for i in range(1, NA) for d in YORDER + (0,)]
     core = [send(g_ref.at[at((1 - c) * HALF + s.start, s.size)], r1.at[s], 0, n, other) for n, s in enumerate(chunks)]
 
     def add(s):
         h[s, :] = g_ref[at(half + s.start, s.size), :] + r1[s, :]
 
-    sums_ya, sums_zb = [], []
-    for n, d in enumerate((1, 3, 2)):
-        core[n].wait_recv()
-        add(chunks[n])
-        sums_ya.append(send(h.at[chunks[n]], r2a.at[d - 1], 1, d - 1, ydev[d]))
-    core[3].wait_recv()
+    def sum_y(i):
+        out = []
+        for d in YORDER:
+            add(ya[i][d])
+            out.append(send(h.at[ya[i][d]], r2a[i].at[d - 1], 6 + i, d - 1, ydev[d]))
+        return out
+
+    def sum_z(i):
+        out = []
+        for d in ZORDER + (0,):
+            s = at(zs[d] * ZA, ZA)
+            t = at(YA * i + zs[d] * ZA, ZA)
+            qa[t, :] = ((h[at(PA * i + y * YA + zs[d] * ZA, ZA), :] + r2a[i][0, s, :])
+                        + (r2a[i][1, s, :] + r2a[i][2, s, :]))
+            if d:
+                out.append(send(qa.at[t], r3a[i].at[d - 1], 6 + NA + i, d - 1, zdev[d]))
+        return out
+
+    came(core[:3])
+    sums_ya = [sum_y(0)]
+    came(core[3:4])
+    sums_zb = []
     for d in ZORDER:
-        s = at(PA + zs[d] * ZB, ZB)
+        s = at(NA * PA + zs[d] * ZB, ZB)
         add(s)
-        sums_zb.append(send(h.at[s], r2b.at[d - 1], 2, d - 1, zdev[d]))
-    add(at(PA + z * ZB, ZB))
-    core[4].wait_recv()
-    add(chunks[4])
-
-    for copy in sums_zb:
-        copy.wait_recv()
-    total = h[at(PA + z * ZB, ZB), :]
+        sums_zb.append(send(h.at[s], r2b.at[d - 1], 1, d - 1, zdev[d]))
+    add(at(NA * PA + z * ZB, ZB))
+    came(core[4:5])
+    add(ya[0][0])
+    came(core[5:])
+    for i in range(1, NA):
+        add(ya[i][0])
+    sums_ya += [sum_y(i) for i in range(1, NA)]
+
+    came(sums_ya[0])
+    sums_za = [sum_z(0)]
+    came(sums_zb)
+    total = h[at(NA * PA + z * ZB, ZB), :]
     for d in range(NZ - 1):
         total = total + r2b[d]
     qb[...] = total
-    sums_yb = [send(qb.at[at(ys[d] * YB, YB)], r3b.at[d - 1], 3, d - 1, ydev[d]) for d in (2, 1, 3)]
-
-    for copy in sums_ya:
-        copy.wait_recv()
-    sums_za = []
-    for d in ZORDER + (0,):
-        s = at(zs[d] * ZA, ZA)
-        qa[s, :] = (h[at(y * YA + zs[d] * ZA, ZA), :] + r2a[0, s, :]) + (r2a[1, s, :] + r2a[2, s, :])
-        if d:
-            sums_za.append(send(qa.at[s], r3a.at[d - 1], 4, d - 1, zdev[d]))
-
-    for copy in sums_yb:
-        copy.wait_recv()
-    mine = at(half + PA + z * ZB + y * YB, YB)
+    sums_yb = [send(qb.at[at(ys[d] * YB, YB)], r3b.at[d - 1], 2, d - 1, ydev[d]) for d in YORDER]
+    for i in range(1, NA):
+        came(sums_ya[i])
+        sums_za.append(sum_z(i))
+
+    came(sums_yb)
+    mine = at(half + NA * PA + z * ZB + y * YB, YB)
     o_ref[mine, :] = (qb[at(y * YB, YB), :] + r3b[0]) + (r3b[1] + r3b[2])
-    back_yb = [send(o_ref.at[mine], o_ref.at[mine], 5, d - 1, ydev[d]) for d in (2, 1, 3)]
-
-    for copy in sums_za:
-        copy.wait_recv()
-    total = qa[at(z * ZA, ZA), :]
-    for d in range(NZ - 1):
-        total = total + r3a[d]
-    mine = at(half + y * YA + z * ZA, ZA)
-    o_ref[mine, :] = total
-    back_za = [send(o_ref.at[mine], o_ref.at[mine], 6, d - 1, zdev[d]) for d in ZORDER]
-
-    for copy in back_yb:
-        copy.wait_recv()
-    own = at(half + PA + z * ZB, ZB)
-    back_zb = [send(o_ref.at[own], o_ref.at[own], 7, d - 1, zdev[d]) for d in ZORDER]
-    for copy in back_za:
-        copy.wait_recv()
-    own = at(half + y * YA, YA)
-    back_ya = [send(o_ref.at[own], o_ref.at[own], 8, d - 1, ydev[d]) for d in (2, 1, 3)]
-    back = [send(o_ref.at[own], o_ref.at[own], 9, 0, other)]
-    for copy in back_zb:
-        copy.wait_recv()
-    part = at(half + PA, PB)
-    back.append(send(o_ref.at[part], o_ref.at[part], 9, 1, other))
-    for n, d in enumerate((2, 1, 3)):
-        back_ya[n].wait_recv()
-        part = at(half + lax.rem(y + NY - d, NY) * YA, YA)
-        back.append(send(o_ref.at[part], o_ref.at[part], 9, 2 + n, other))
-    for copy in back:
-        copy.wait_recv()
+    back_yb = [send(o_ref.at[mine], o_ref.at[mine], 3, d - 1, ydev[d]) for d in YORDER]
+
+    back_za = []
+    for i in range(NA):
+        came(sums_za[i])
+        total = qa[at(YA * i + z * ZA, ZA), :]
+        for d in range(NZ - 1):
+            total = total + r3a[i][d]
+        mine = at(half + PA * i + y * YA + z * ZA, ZA)
+        o_ref[mine, :] = total
+        back_za.append([send(o_ref.at[mine], o_ref.at[mine], 6 + 2 * NA + i, d - 1, zdev[d]) for d in ZORDER])
+
+    back_ya, back = [], []
+    for i in range(NA):
+        came(back_za[i])
+        own = at(half + PA * i + y * YA, YA)
+        back_ya.append([send(o_ref.at[own], o_ref.at[own], 6 + 3 * NA + i, d - 1, ydev[d]) for d in YORDER])
+        back.append(send(o_ref.at[own], o_ref.at[own], 5, 4 * i, other))
+    came(back_yb)
+    own = at(half + NA * PA + z * ZB, ZB)
+    back_zb = [send(o_ref.at[own], o_ref.at[own], 4, d - 1, zdev[d]) for d in ZORDER]
+    for i in range(NA):
+        for n, d in enumerate(YORDER):
+            back_ya[i][n].wait_recv()
+            part = at(half + PA * i + lax.rem(y + NY - d, NY) * YA, YA)
+            back.append(send(o_ref.at[part], o_ref.at[part], 5, 4 * i + 1 + n, other))
+    came(back_zb)
+    part = at(half + NA * PA, PB)
+    back.append(send(o_ref.at[part], o_ref.at[part], 5, 4 * NA, other))
+    came(back)
     for copy in sent:
         copy.wait_send()
 
 
 def comm(g):
-    counts = (5, 3, 7, 3, 7, 3, 7, 7, 3, 5)
-    buffers = ((HALF,), (HALF,), (3, YA), (7, ZB), (YA,), (ZB,), (7, ZA), (3, YB))
+    counts = (4 * NA + 1, 7, 3, 3, 7, 4 * NA + 1) + (3,) * NA + (7,) * (2 * NA) + (3,) * NA
+    buffers = ((HALF,), (HALF,), (NA * YA,), (ZB,)) + ((3, YA),) * NA + ((7, ZA),) * NA + ((7, ZB), (3, YB))
     return pl.pallas_call(
         comm_kern,
         out_shape=jax.ShapeDtypeStruct((2 * HALF, 128), F32),
@@ -393,43 +417,49 @@
         name="comm")(g)
 
 
-def swap_kern(n_blocks, t_ref, x_ref, o_ref, mid, out, ss1, rs1, ss2, rs2):
+def swap_kern(n_blocks, t_ref, x_ref, o_ref, *rest):
+    mids, outs, (ss1, rs1, ss2, rs2) = rest[:NS], rest[NS:2 * NS], rest[2 * NS:]
     me = lax.axis_index("pair")
     others = [lax.rem(me + d, 4) for d in range(4)]
     barrier = pltpu.get_barrier_semaphore()
     for d in (2, 1, 3):
         pl.semaphore_signal(barrier, inc=1, device_id={"pair": others[d]}, device_id_type=MESH)
     pl.semaphore_wait(barrier, 3)
-
-    def rows(j):
-        return pl.ds(pl.multiple_of(64 * j, 64), 64)
-
-    def send(src, dst, ss, rs, d):
+    size = 64 // NS
+
+    def rows(j, i):
+        return pl.ds(pl.multiple_of(64 * j + size * i, size), size)
+
+    def send(src, dst, ss, rs, i, d):
         copy = pltpu.make_async_remote_copy(
-            src_ref=src, dst_ref=dst, send_sem=ss.at[d - 1], recv_sem=rs.at[d - 1],
+            src_ref=src, dst_ref=dst, send_sem=ss.at[i, d - 1], recv_sem=rs.at[i, d - 1],
             device_id={"pair": others[d]}, device_id_type=MESH)
         copy.start()
         return copy
 
-    there = [send(x_ref.at[:, rows(others[d]), :], mid.at[:, me], ss1, rs1, d) for d in (2, 1, 3)]
-    mid[:, me] = x_ref[:, rows(me), :]
-    for copy in there:
-        copy.wait_recv()
+    there = [[send(x_ref.at[:, rows(others[d], i), :], mids[i].at[:, me], ss1, rs1, i, d) for d in (2, 1, 3)]
+             for i in range(NS)]
+    for i in range(NS):
+        mids[i][:, me] = x_ref[:, rows(me, i), :]
     back = []
-    for d in (2, 1, 3, 0):
-        for n in range(n_blocks):
-            at = t_ref[8 + n_blocks * others[d] + n] if n_blocks == 2 else t_ref[others[d]]
-            block = mid[at // 4, at % 4]
+    for i in range(NS):
+        for copy in there[i]:
+            copy.wait_recv()
+        for d in (2, 1, 3, 0):
+            for n in range(n_blocks):
+                at = t_ref[8 + n_blocks * others[d] + n] if n_blocks == 2 else t_ref[others[d]]
+                block = mids[i][at // 4, at % 4]
+                if d:
+                    outs[i][d - 1, :, 512 * n:512 * n + 512] = block
+                else:
+                    o_ref[rows(me, i), 512 * n:512 * n + 512] = block
             if d:
-                out[d - 1, :, 512 * n:512 * n + 512] = block
-            else:
-                o_ref[rows(me), 512 * n:512 * n + 512] = block
-        if d:
-            back.append(send(out.at[d - 1], o_ref.at[rows(me), :], ss2, rs2, d))
+                back.append(send(outs[i].at[d - 1], o_ref.at[rows(me, i), :], ss2, rs2, i, d))
     for copy in back:
         copy.wait_recv()
-    for copy in there + back:
-        copy.wait_send()
+    for copies in there + [back]:
+        for copy in copies:
+            copy.wait_send()
 
 
 def swap(t, x):
@@ -440,8 +470,8 @@
         out_shape=jax.ShapeDtypeStruct((256, 512 * n), F32),
         in_specs=[pl.BlockSpec(memory_space=pltpu.SMEM), vm],
         out_specs=vm,
-        scratch_shapes=[pltpu.VMEM((n, 4, 64, 512), F32), pltpu.VMEM((3, 64, 512 * n), F32)]
-        + [pltpu.SemaphoreType.DMA((3,))] * 4,
+        scratch_shapes=[pltpu.VMEM((n, 4, 64 // NS, 512), F32)] * NS + [pltpu.VMEM((3, 64 // NS, 512 * n), F32)] * NS
+        + [pltpu.SemaphoreType.DMA((NS, 3))] * 4,
         compiler_params=pltpu.CompilerParams(
             vmem_limit_bytes=16 * 2**20, collective_id=n, has_side_effects=True),
         name="swap")(t, x)

time: 217 us -> 205 us (0.945)
  Pallas kernels: 214 us -> 202 us
    pallas_call x2, Pallas kernels: 86.3 us -> 77.8 us  [comm(): pl.pallas_call(comm_kern, out_shape=jax.ShapeDtypeStruct((2 * HALF, 128),...]
    pallas_call x2, Pallas kernels: 48.2 us -> 44.3 us  [swap(): pl.pallas_call(functools.partial(swap_kern, n), out_shape=jax.ShapeDtypeS...]
where the time goes in v2:
time: 205 us
  Pallas kernels  202 us (99%)
  local copies, waits for them, and re-layouts  2.88 us (1%)
    pallas_call x4, Pallas kernels, vmem_call(): pl.pallas_call(kern, out_shape=outs, in_specs=[sm] * n_smem + [vm] * (len...  79.8 us
    pallas_call x2, Pallas kernels, comm(): pl.pallas_call(comm_kern, out_shape=jax.ShapeDtypeStruct((2 * HALF, 128),...  77.8 us
    pallas_call x2, Pallas kernels, swap(): pl.pallas_call(functools.partial(swap_kern, n), out_shape=jax.ShapeDtypeS...  44.3 us

profile of v2, /device:TPU:1, one launch (start us, length us, event | category | flops | bytes accessed | tf_op | source)
XLA Modules:
  0.0 204.9 jit_solution(9908776480436574630)
XLA Ops:
  0.0 0.0 copy-start
  0.0 1.2 copy-done
  1.2 0.0 copy-start.2
  1.2 0.7 copy-done.2
  1.9 2.5 %gram.2 = (f32[4096,128]{1,0:T(8,128)S(1)}, s32[16]{0:T(128)S(1)}) custom-call(s32[2,8]{1,0:T(2,128)S(1)} %copy-done.2, f32[256,1024]{1,0:T(8,128)S(1)} %copy-done), custom_call_target="tpu_custom_call" | custom-call | tf_op jit(solution)/shard_map/gram/pallas_call | solution.py:40
  4.4 0.0 copy-start.1
  4.4 41.6 %comm.2.g_ref = f32[4096,128]{1,0:T(8,128)S(1)} custom-call(f32[4096,128]{1,0:T(8,128)S(1)} %get-tuple-element.10.g_ref), custom_call_target="tpu_custom_call" | custom-call | tf_op jit(solution)/shard_map/comm/pallas_call | solution.py:408
  46.0 0.0 copy-done.1
  46.1 37.6 %solve.2 = (f32[256,512]{1,0:T(8,128)S(1)}, f32[256,512]{1,0:T(8,128)S(1)}) custom-call(s32[16]{0:T(128)S(1)} %get-tuple-element.9.t_ref, f32[4096,128]{1,0:T(8,128)S(1)} %comm.2.g_ref, f32[256,1024]{1,0:T(8,128)S(1)} %copy-done.1), custom_call_target="tpu_custom_call" | custom-call | tf_op jit(solution)/shard_map/solve/pallas_call | solution.py:40
  83.7 16.7 %swap.2.refs_1_ = f32[256,512]{1,0:T(8,128)S(1)} custom-call(s32[16]{0:T(128)S(1)} %get-tuple-element.9.t_ref, f32[1,256,512]{2,1,0:T(8,128)S(1)} %bitcast.1), custom_call_target="tpu_custom_call" | custom-call | tf_op jit(solution)/shard_map/swap/pallas_call | solution.py:468
  100.4 1.8 gram.3.g_ref
  102.2 36.2 %comm.3.g_ref = f32[4096,128]{1,0:T(8,128)S(1)} custom-call(f32[4096,128]{1,0:T(8,128)S(1)} %gram.3.g_ref), custom_call_target="tpu_custom_call" | custom-call | tf_op jit(solution)/shard_map/comm/pallas_call | solution.py:408
  138.4 37.9 %solve.3.x_ref = f32[2,256,512]{2,1,0:T(8,128)S(1)} custom-call(s32[16]{0:T(128)S(1)} %get-tuple-element.9.t_ref, f32[4096,128]{1,0:T(8,128)S(1)} %comm.3.g_ref, f32[256,512]{1,0:T(8,128)S(1)} %get-tuple-element.11.refs_0_, f32[256,512]{1,0:T(8,128)S(1)} %swap.2.refs_1_), custom_call_target="tpu_custom_call" | custom-call | tf_op jit(solution)/shard_map/solve/pallas_call | solution.py:40
  176.3 27.6 %swap.3 = f32[256,1024]{1,0:T(8,128)S(1)} custom-call(s32[16]{0:T(128)S(1)} %get-tuple-element.9.t_ref, f32[2,256,512]{2,1,0:T(8,128)S(1)} %solve.3.x_ref), custom_call_target="tpu_custom_call" | custom-call | tf_op jit(solution)/shard_map/swap/pallas_call | solution.py:468
  203.9 1.0 copy.4
Async XLA Ops:
  0.0 1.2 copy-start
  1.2 0.7 copy-start.2
  4.4 41.6 %copy-start.1 = (f32[256,1024]{1,0:T(8,128)S(1)}, f32[256,1024]{1,0:T(8,128)}, u32[]{:S(2)}) copy-start(f32[256,1024]{1,0:T(8,128)} %refs_0_.3) | copy-start | bytes 3145732

commit v3 on v2

--- a/solution.py
+++ b/solution.py
@@ -321,7 +321,9 @@
 
     def sum_y(i):
         out = []
-        for d in YORDER:
+        for n, d in enumerate(YORDER):
+            if i == 0:
+                came(core[n:n + 1])
             add(ya[i][d])
             out.append(send(h.at[ya[i][d]], r2a[i].at[d - 1], 6 + i, d - 1, ydev[d]))
         return out
@@ -337,7 +339,6 @@
                 out.append(send(qa.at[t], r3a[i].at[d - 1], 6 + NA + i, d - 1, zdev[d]))
         return out
 
-    came(core[:3])
     sums_ya = [sum_y(0)]
     came(core[3:4])
     sums_zb = []

time: 205 us -> 204 us (level)
  no operation moved by 1% of the time
where the time goes in v3:
time: 204 us
  Pallas kernels  201 us (99%)
  local copies, waits for them, and re-layouts  2.88 us (1%)
    pallas_call x4, Pallas kernels, vmem_call(): pl.pallas_call(kern, out_shape=outs, in_specs=[sm] * n_smem + [vm] * (len...  79.8 us
    pallas_call x2, Pallas kernels, comm(): pl.pallas_call(comm_kern, out_shape=jax.ShapeDtypeStruct((2 * HALF, 128),...  77.4 us
    pallas_call x2, Pallas kernels, swap(): pl.pallas_call(functools.partial(swap_kern, n), out_shape=jax.ShapeDtypeS...  43.8 us

profile of v3, /device:TPU:1, one launch (start us, length us, event | category | flops | bytes accessed | tf_op | source)
XLA Modules:
  0.0 204.0 jit_solution(57693532737999556)
XLA Ops:
  0.0 0.0 copy-start
  0.0 1.2 copy-done
  1.2 0.0 copy-start.2
  1.2 0.7 copy-done.2
  1.9 2.5 %gram.2 = (f32[4096,128]{1,0:T(8,128)S(1)}, s32[16]{0:T(128)S(1)}) custom-call(s32[2,8]{1,0:T(2,128)S(1)} %copy-done.2, f32[256,1024]{1,0:T(8,128)S(1)} %copy-done), custom_call_target="tpu_custom_call" | custom-call | tf_op jit(solution)/shard_map/gram/pallas_call | solution.py:40
  4.4 0.0 copy-start.1
  4.4 41.2 %comm.2.g_ref = f32[4096,128]{1,0:T(8,128)S(1)} custom-call(f32[4096,128]{1,0:T(8,128)S(1)} %get-tuple-element.10.g_ref), custom_call_target="tpu_custom_call" | custom-call | tf_op jit(solution)/shard_map/comm/pallas_call | solution.py:409
  45.6 0.0 copy-done.1
  45.6 37.6 %solve.2 = (f32[256,512]{1,0:T(8,128)S(1)}, f32[256,512]{1,0:T(8,128)S(1)}) custom-call(s32[16]{0:T(128)S(1)} %get-tuple-element.9.t_ref, f32[4096,128]{1,0:T(8,128)S(1)} %comm.2.g_ref, f32[256,1024]{1,0:T(8,128)S(1)} %copy-done.1), custom_call_target="tpu_custom_call" | custom-call | tf_op jit(solution)/shard_map/solve/pallas_call | solution.py:40
  83.2 16.8 %swap.2.refs_1_ = f32[256,512]{1,0:T(8,128)S(1)} custom-call(s32[16]{0:T(128)S(1)} %get-tuple-element.9.t_ref, f32[1,256,512]{2,1,0:T(8,128)S(1)} %bitcast.1), custom_call_target="tpu_custom_call" | custom-call | tf_op jit(solution)/shard_map/swap/pallas_call | solution.py:469
  100.0 1.8 gram.3.g_ref
  101.9 36.3 %comm.3.g_ref = f32[4096,128]{1,0:T(8,128)S(1)} custom-call(f32[4096,128]{1,0:T(8,128)S(1)} %gram.3.g_ref), custom_call_target="tpu_custom_call" | custom-call | tf_op jit(solution)/shard_map/comm/pallas_call | solution.py:409
  138.2 37.8 %solve.3.x_ref = f32[2,256,512]{2,1,0:T(8,128)S(1)} custom-call(s32[16]{0:T(128)S(1)} %get-tuple-element.9.t_ref, f32[4096,128]{1,0:T(8,128)S(1)} %comm.3.g_ref, f32[256,512]{1,0:T(8,128)S(1)} %get-tuple-element.11.refs_0_, f32[256,512]{1,0:T(8,128)S(1)} %swap.2.refs_1_), custom_call_target="tpu_custom_call" | custom-call | tf_op jit(solution)/shard_map/solve/pallas_call | solution.py:40
  176.0 27.0 %swap.3 = f32[256,1024]{1,0:T(8,128)S(1)} custom-call(s32[16]{0:T(128)S(1)} %get-tuple-element.9.t_ref, f32[2,256,512]{2,1,0:T(8,128)S(1)} %solve.3.x_ref), custom_call_target="tpu_custom_call" | custom-call | tf_op jit(solution)/shard_map/swap/pallas_call | solution.py:469
  203.0 1.0 copy.4
Async XLA Ops:
  0.0 1.2 copy-start
  1.2 0.7 copy-start.2
  4.4 41.2 %copy-start.1 = (f32[256,1024]{1,0:T(8,128)S(1)}, f32[256,1024]{1,0:T(8,128)}, u32[]{:S(2)}) copy-start(f32[256,1024]{1,0:T(8,128)} %refs_0_.3) | copy-start | bytes 3145732
